TPU v7x, 32 devices: a whole 2x2x4 slice. The times are simulated.
32 devices in a mesh: tile: 8 (over z, y), day: 4 (over x, core).
Axes of the slice: x: 2, y: 2, z: 4, core: 2. Of those that a mesh axis runs over, the one named last changes fastest.
Arguments:
- coarse: bfloat16 [8, 20, 128, 256], P('day', None, 'tile'), may hold values from -6 to 6
- fine: bfloat16 [8, 4, 2048, 4096], P('day', None, 'tile'), may hold values from -6 to 6
- coarse_lat: bfloat16 [128, 64], P('tile'), may hold values from -0.5 to 0.5
- coarse_lon: bfloat16 [256, 64], replicated, may hold values from -0.375 to 0.375
- coarse_var: bfloat16 [20, 8], replicated, may hold values from -1.25 to 1.25
- fine_lat: bfloat16 [2048, 64], P('tile'), may hold values from -0.75 to 0.75
- fine_lon: bfloat16 [4096, 64], replicated, may hold values from -0.75 to 0.75
- fine_var: bfloat16 [4, 8], replicated, may hold values from -2 to 2
Outputs:
- grad_fine_lat: float32 [2048, 64], P('tile')
- grad_fine_lon: float32 [4096, 64], P('tile')
- grad_fine_var: float32 [4, 8], replicated
- grad_coarse_lat: float32 [128, 64], P('tile')
- grad_coarse_lon: float32 [256, 64], replicated
- grad_coarse_var: float32 [20, 8], replicated
All inputs are finite; a program needn't handle non-finite values.
Results may differ from a plain program's by a relative error of at most 0.00065.
Values sent between devices are 32-bit elements; how exact they have to be, the bound alone decides.
A program may use at most 128 MiB of HBM per device.

v0:
```python
import math

import jax
import jax.numpy as jnp
from jax import lax
from jax.sharding import PartitionSpec as P

R1 = 64
R2 = 64
R3 = 8
F1 = 2048
F2 = 4096
F3 = 4


HIGHEST = lax.Precision.HIGHEST


def rows_by_factor(matrix, factor):
    return lax.dot_general(
        matrix, factor, (((1,), (1,)), ((), ())), preferred_element_type=jnp.float32
    )


def outer_rows(left, right):
    return lax.dot_general(
        left, right, (((0,), (0,)), ((), ())), preferred_element_type=jnp.float32
    )


def per_device(coarse, fine, coarse_lat, coarse_lon, coarse_var, fine_lat, fine_lon, fine_var):
    days_here, chans, lats, lons = coarse.shape
    lat_float = coarse_lat.astype(jnp.float32)
    var_float = coarse_var.astype(jnp.float32)
    fine_lat_float = fine_lat.astype(jnp.float32)
    fine_var_float = fine_var.astype(jnp.float32)
    along = jnp.dot(coarse.reshape(-1, lons), coarse_lon, preferred_element_type=jnp.float32)
    along = along.reshape(days_here, chans, lats, coarse_lon.shape[1])
    core_part = jnp.einsum("ncar,as,ct->nsrt", along, lat_float, var_float, precision=HIGHEST)
    core = lax.psum(core_part, "tile")
    mixed = jnp.einsum("is,nsrt->nirt", fine_lat_float, core, precision=HIGHEST)
    lifted = jnp.einsum("nirt,vt->nvir", mixed, fine_var_float, precision=HIGHEST).astype(
        jnp.bfloat16
    )
    flat_lifted = lifted.reshape(-1, lifted.shape[3])
    predicted = rows_by_factor(flat_lifted, fine_lon)
    target = fine.reshape(predicted.shape).astype(jnp.float32)
    residual = (predicted - target).astype(jnp.bfloat16)
    back = jnp.dot(residual, fine_lon, preferred_element_type=jnp.float32).reshape(lifted.shape)
    grad_lon_tile = outer_rows(residual, flat_lifted)
    grad_lat_fine = jnp.einsum("nvir,nsrt,vt->is", back, core, fine_var_float, precision=HIGHEST)
    grad_var_fine = jnp.einsum("nvir,nirt->vt", back, mixed, precision=HIGHEST)
    day_grads = jnp.einsum(
        "nvir,is,vt->nsrt", back, fine_lat_float, fine_var_float, precision=HIGHEST
    )
    core_grad = lax.psum(day_grads, "tile") * math.sqrt(R1 * R2 * R3 / (F1 * F2 * F3))
    grad_first_coarse = jnp.einsum(
        "ncar,ct,nsrt->as", along, var_float, core_grad, precision=HIGHEST
    )
    flipped = jnp.transpose(coarse, (0, 1, 3, 2)).reshape(-1, lats)
    lat_coarse = jnp.dot(flipped, coarse_lat, preferred_element_type=jnp.float32)
    lat_coarse = lat_coarse.reshape(days_here, chans, lons, coarse_lat.shape[1])
    weighted = jnp.einsum("ct,nsrt->ncsr", var_float, core_grad, precision=HIGHEST)
    grad_second_coarse = jnp.einsum("ncbs,ncsr->br", lat_coarse, weighted, precision=HIGHEST)
    grad_third_coarse = jnp.einsum(
        "ncar,as,nsrt->ct", along, lat_float, core_grad, precision=HIGHEST
    )
    summed_lon, summed_var, summed_fine_var = lax.psum(
        (grad_second_coarse, grad_third_coarse, grad_var_fine), ("tile", "day")
    )
    summed_lat, summed_coarse_lat, whole_lon = lax.psum(
        (grad_lat_fine, grad_first_coarse, grad_lon_tile), "day"
    )
    owned_lon = lax.psum_scatter(whole_lon, "tile", scatter_dimension=0, tiled=True)
    days = days_here * lax.axis_size("day")
    return (
        summed_lat / math.sqrt(days * F3 * F2),
        owned_lon / math.sqrt(days * F3 * F1),
        summed_fine_var / math.sqrt(days * F1 * F2),
        summed_coarse_lat / math.sqrt(days * R2 * R3),
        summed_lon / math.sqrt(days * R1 * R3),
        summed_var / math.sqrt(days * R1 * R2),
    )


def solution(mesh):
    in_specs = (
        P("day", None, "tile", None),
        P("day", None, "tile", None),
        P("tile", None),
        P(),
        P(),
        P("tile", None),
        P(),
        P(),
    )
    out_specs = (P("tile", None), P("tile", None), P(), P("tile", None), P(), P())
    return jax.shard_map(
        per_device, mesh=mesh, in_specs=in_specs, out_specs=out_specs, check_vma=False
    )
```

profile of v0, /device:TPU:0, one launch (start us, length us, event | category | flops | bytes accessed | tf_op | source)
XLA Modules:
  0.0 433.1 jit_solution(16536955555524402023)
XLA Ops:
  7.2 0.0 copy-start
  7.2 0.0 all-reduce.7.cloned.1.call-start
  7.2 1.2 fusion.24
  8.5 1.0 convolution_bitcast_fusion.3
  9.5 0.0 copy-start.2
  9.5 0.6 copy-done.2
  10.2 2.1 convolution_bitcast_fusion.2
  12.3 0.0 all-reduce.7.cloned.1.call-update
  12.3 0.0 all-reduce.9.cloned.1.call-start
  12.3 1.5 fusion.16
  13.9 73.7 %all-reduce.7.cloned.1.call-done = f32[2,64,64,8]{1,2,0,3:T(8,128)} async-done(((f32[2,64,64,8]{1,2,0,3:T(8,128)}), f32[2,64,64,8]{1,2,0,3:T(8,128)}) %all-reduce.7.cloned.1.call-update) | async-done | bytes 262160 | tf_op jit(solution)/shard_map/psum | solution.py:40
  87.5 1.8 convolution_bitcast_fusion
  89.4 0.0 copy-start.1
  89.4 1.0 copy-done.1
  90.4 1.3 fusion.3
  91.7 0.8 copy.25
  92.5 1.8 reshape.29
  94.3 0.0 copy-done
  94.3 11.6 %fusion = bf16[2048,4096]{1,0:T(8,128)(2,1)} fusion(bf16[2,4,256,4096]{3,2,1,0:T(8,128)(2,1)} %param.9, bf16[2048,64]{0,1:T(8,128)(2,1)} %reshape.29, bf16[4096,64]{0,1:T(8,128)(2,1)S(1)} %copy-done), kind=kOutput, calls=%fused_computation.1 | convolution fusion | flops 1098907648 | bytes 34340864 | tf_op jit(solution)/shard_map/dot_general | solution.py:20
  105.9 0.0 copy-start.3
  105.9 0.0 copy-start.5
  105.9 11.8 %fusion.38 = f32[2048,64]{0,1:T(8,128)} fusion(bf16[2048,4096]{1,0:T(8,128)(2,1)} %fusion, bf16[4096,64]{0,1:T(8,128)(2,1)S(1)} %copy-done), kind=kOutput, calls=%fused_computation.53 | convolution fusion | flops 1073741824 | bytes 17825792 | tf_op jit(solution)/shard_map/dot_general | solution.py:49
  117.6 2.2 reshape.30
  119.8 0.0 copy-done.3
  119.8 0.0 copy-start.4
  119.9 2.2 fusion.11
  122.1 1.8 copy.40
  123.9 0.0 copy-done.5
  123.9 2.1 convolution_bitcast_fusion.1
  126.0 0.0 copy-start.6
  126.0 0.0 all-reduce.9.cloned.1.call-update
  126.1 0.2 reduce-scatter.2.cloned.1.call-start
  126.3 10.0 %fusion.39 = f32[4096,64]{0,1:T(8,128)} fusion(bf16[2048,64]{0,1:T(8,128)(2,1)} %reshape.29, bf16[2048,4096]{1,0:T(8,128)(2,1)} %fusion), kind=kOutput, calls=%fused_computation.54 | convolution fusion | flops 1073741824 | bytes 18087936 | tf_op jit(solution)/shard_map/dot_general | solution.py:26
  136.3 0.0 reduce-scatter.2.cloned.1.call-update
  136.3 0.0 all-reduce.11.cloned.1.call-start
  136.3 2.0 copy.36
  138.4 2.1 fusion.35
  140.5 3.9 convolution_bitcast_fusion.7
  144.4 53.5 %all-reduce.9.cloned.1.call-done = f32[2,64,64,8]{2,3,0,1:T(8,128)} async-done(((f32[2,64,64,8]{2,3,0,1:T(8,128)}), f32[2,64,64,8]{2,3,0,1:T(8,128)}) %all-reduce.9.cloned.1.call-update) | async-done | bytes 262160 | tf_op jit(solution)/shard_map/psum | solution.py:56
  197.9 1.9 broadcast_multiply_fusion
  199.7 2.1 copy.46
  201.8 0.0 copy-done.4
  201.8 1.8 fusion.28
  203.6 0.6 convolution_bitcast_fusion.6
  204.2 2.3 convolution_bitcast_fusion.4
  206.5 40.0 %all-reduce = (f32[4,8]{1,0:T(4,128)S(1)}, f32[20,8]{0,1:T(8,128)S(1)}) all-reduce(f32[4,8]{1,0:T(4,128)S(1)} %convolution_bitcast_fusion.7, f32[20,8]{0,1:T(8,128)S(1)} %convolution_bitcast_fusion.6), channel_id=1, replica_groups=mesh['tile'=8,'day'=4] {'tile','day'}, use_global_device_ids=true, to_apply=%region_4.0 | all-reduce | flops 192 | bytes 1536 | tf_op jit(solution)/shard_map/psum | solution.py:68
  246.5 0.0 copy-done.6
  246.5 3.0 fusion.7
  249.5 2.9 copy.44
  252.4 1.5 convolution_bitcast_fusion.5
  253.9 5.9 %psum.61 = f32[16,64]{1,0:T(8,128)S(1)} all-reduce(f32[16,64]{1,0:T(8,128)S(1)} %convolution_bitcast_fusion.5), channel_id=1, replica_groups=mesh['tile'=8,'day'=4] {'day'}, use_global_device_ids=true, to_apply=%region_6.0 | all-reduce | flops 1024 | bytes 8192 | tf_op jit(solution)/shard_map/psum | solution.py:71
  259.8 0.6 broadcast_multiply_fusion.5
  260.4 0.6 broadcast_multiply_fusion.4
  261.0 3.6 fusion.4
  264.6 0.0 all-reduce.11.cloned.1.call-update
  264.6 0.0 all-reduce.13.cloned.1.call-start
  264.6 0.6 broadcast_multiply_fusion.6
  265.2 0.0 reduce-scatter.2.cloned.1.call-done
  265.2 0.0 all-reduce.13.cloned.1.call-update
  265.2 122.8 %all-reduce.11.cloned.1.call-done = f32[256,64]{0,1:T(8,128)} async-done(((f32[256,64]{0,1:T(8,128)}), f32[256,64]{0,1:T(8,128)}) %all-reduce.11.cloned.1.call-update) | async-done | bytes 65552 | tf_op jit(solution)/shard_map/psum | solution.py:68
  388.1 1.5 broadcast_multiply_fusion.2
  389.6 34.0 %all-reduce.13.cloned.1.call-done = (f32[256,64]{0,1:T(8,128)}, f32[512,64]{0,1:T(8,128)}) async-done(((f32[256,64]{0,1:T(8,128)}, f32[512,64]{0,1:T(8,128)}), (f32[256,64]{0,1:T(8,128)}, f32[512,64]{0,1:T(8,128)})) %all-reduce.13.cloned.1.call-update) | async-done | bytes 196624 | tf_op jit(solution)/shard_map/psum | solution.py:71
  423.6 1.5 broadcast_multiply_fusion.3
  425.0 1.6 broadcast_multiply_fusion.1
Async XLA Ops:
  7.2 87.2 %copy-start = (bf16[4096,64]{0,1:T(8,128)(2,1)S(1)}, bf16[4096,64]{0,1:T(8,128)(2,1)}, u32[]{:S(2)}) copy-start(bf16[4096,64]{0,1:T(8,128)(2,1)} %param.14) | copy-start | bytes 1572868
  7.2 80.4 %all-reduce.7.cloned.1.call-start = ((), (), s32[]{:S(2)}) async-start(), calls=%async_computation.1 | async-start | bytes 1048576 | tf_op jit(solution)/shard_map/psum | solution.py:40
  9.5 0.7 copy-start.2
  12.3 185.6 %all-reduce.9.cloned.1.call-start = ((), (), s32[]{:S(2)}) async-start(), calls=%async_computation.2 | async-start | bytes 1048576 | tf_op jit(solution)/shard_map/psum | solution.py:56
  89.4 1.0 copy-start.1
  105.9 14.0 %copy-start.3 = (bf16[256,64]{0,1:T(8,128)(2,1)S(1)}, bf16[256,64]{0,1:T(8,128)(2,1)}, u32[]{:S(2)}) copy-start(bf16[256,64]{0,1:T(8,128)(2,1)} %param.13) | copy-start | bytes 98308
  105.9 18.0 %copy-start.5 = (bf16[4,8]{1,0:T(4,128)(2,1)S(1)}, bf16[4,8]{1,0:T(4,128)(2,1)}, u32[]{:S(2)}) copy-start(bf16[4,8]{1,0:T(4,128)(2,1)} %param.15) | copy-start | bytes 196
  119.8 82.0 %copy-start.4 = (bf16[16,64]{1,0:T(8,128)(2,1)S(1)}, bf16[16,64]{1,0:T(8,128)(2,1)}, u32[]{:S(2)}) copy-start(bf16[16,64]{1,0:T(8,128)(2,1)} %param.10) | copy-start | bytes 6148
  126.0 120.5 %copy-start.6 = (bf16[20,8]{0,1:T(8,128)(2,1)S(1)}, bf16[20,8]{0,1:T(8,128)(2,1)}, u32[]{:S(2)}) copy-start(bf16[20,8]{0,1:T(8,128)(2,1)} %param.12) | copy-start | bytes 964
  126.1 139.2 %reduce-scatter.2.cloned.1.call-start = ((), (), s32[]{:S(2)}) async-start(), calls=%async_computation.4 | async-start | bytes 1179648 | tf_op jit(solution)/shard_map/reduce_scatter | solution.py:74
  136.3 251.8 %all-reduce.11.cloned.1.call-start = ((), (), s32[]{:S(2)}) async-start(), calls=%async_computation.3 | async-start | bytes 131072 | tf_op jit(solution)/shard_map/psum | solution.py:68
  264.6 159.0 %all-reduce.13.cloned.1.call-start = ((), (), s32[]{:S(2)}) async-start(), calls=%async_computation.5 | async-start | bytes 393216 | tf_op jit(solution)/shard_map/psum | solution.py:71
Sparse Core Ops, SparseCore 0:
  12.4 75.0 all-reduce.6
  126.2 71.6 all-reduce.8
  201.3 63.2 reduce-scatter.1
  271.5 116.5 all-reduce.10
  391.0 32.5 all-reduce.12
where the time goes:
time: 434 us; the launch traced here: 433 us
  waiting for transfers between devices  284 us (65%)
  matrix products  65.5 us (15%)
  blocking collectives  45.9 us (11%)
  local copies, waits for them, and re-layouts  15.3 us (4%)
  between operations  13.9 us (3%)
  other arithmetic  8.16 us (2%)
    psum x1, waiting for transfers between devices, per_device(): lax.psum((grad_second_coarse, grad_third_coarse, grad_var_fine), ('tile',...  123 us
    psum x1, waiting for transfers between devices, per_device(): core = lax.psum(core_part, 'tile')  73.7 us
    psum x1, waiting for transfers between devices, per_device(): lax.psum(day_grads, 'tile') * math.sqrt(R1 * R2 * R3 / (F1 * F2 * F3))  53.5 us
    psum x1, blocking collectives, per_device(): lax.psum((grad_second_coarse, grad_third_coarse, grad_var_fine), ('tile',...  40 us
    psum x1, waiting for transfers between devices, per_device(): lax.psum((grad_lat_fine, grad_first_coarse, grad_lon_tile), 'day')  34 us
    dot_general x1, matrix products, per_device(): jnp.dot(residual, fine_lon, preferred_element_type=jnp.float32)  11.8 us
    dot_general x1, matrix products, rows_by_factor(): lax.dot_general(matrix, factor, (((1,), (1,)), ((), ())), preferred_eleme...  11.6 us
    dot_general x1, matrix products, outer_rows(): lax.dot_general(left, right, (((0,), (0,)), ((), ())), preferred_element_...  9.99 us
  transfers between devices with their start and end apart: 5, of which 4 were waited for; matrix products, arithmetic and copies ran while one was open for 10% of the time, Pallas kernels for 0%

commit v1 on v0

v1 whole, which is shorter than its diff:
```python
import functools
import math

import jax
import jax.numpy as jnp
from jax import lax
from jax.experimental import pallas as pl
from jax.experimental.pallas import tpu as pltpu
from jax.sharding import PartitionSpec as P

F32 = jnp.float32
BF16 = jnp.bfloat16
MESH = pl.DeviceIdType.MESH
LANES = 128


def dot(left, right):
    return jnp.dot(left, right, preferred_element_type=F32)


def dot_nt(left, right):
    return lax.dot_general(left, right, (((1,), (1,)), ((), ())), preferred_element_type=F32)


def halves(value):
    high = value.astype(BF16)
    return high, (value - high.astype(F32)).astype(BF16)


def dot_exact(left, right):
    high, low = halves(right)
    return dot(left, high) + dot(left, low)


def dot_nt_three(left, right):
    lh, ll = halves(left)
    rh, rl = halves(right)
    return dot_nt(lh, rh) + (dot_nt(lh, rl) + dot_nt(ll, rh))


def kernel(
    d,
    cvar, fvar, coarse, clat, clon, flat, flon, fine,
    o_flat, o_flon, o_fin, o_small, o_clat,
    fbuf, along, wall, wfl, core, mixed, lifted, lifted_t, lon_pad, lon_pad_t,
    back, spread, fva, gl, gday, gown, gtile, gfin,
    qsend, qrecv, vv, xs, lat_day, clat_day, fsend, frecv, fday, fall,
    s_fine, s_w, r_w, s_q, r_q, s_gd, r_gd, s_gt, r_gt, s_gf, r_gf,
    s_ld, r_ld, s_cd, r_cd, s_fs, r_fs, s_fd, r_fd, s_fa, r_fa,
):
    T, DAY, N, C, A, R, S, TR, V, I, J = (
        d["T"], d["DAY"], d["N"], d["C"], d["A"], d["R"], d["S"], d["TR"], d["V"], d["I"], d["J"]
    )
    JB, NB, NSUB, jb, rq, rr = d["JB"], d["NB"], d["NSUB"], d["jb"], d["rq"], d["rr"]
    L = N * R
    me = lax.axis_index("tile")
    day = lax.axis_index("day")
    first = lax.rem(lax.div(me * jb, JB) + 1, NB)

    def block_of(k):
        return lax.rem(first + k, NB)

    def fine_copy(k):
        columns = pl.ds(pl.multiple_of(block_of(k) * JB, JB), JB)
        return pltpu.make_async_copy(fine.at[:, :, :, columns], fbuf.at[k], s_fine.at[k])

    @pl.loop(0, NB)
    def _(k):
        fine_copy(k).start()

    barrier = pltpu.get_barrier_semaphore()

    @pl.loop(1, T)
    def _(off):
        pl.semaphore_signal(barrier, inc=1, device_id={"tile": lax.rem(me + off, T)}, device_id_type=MESH)

    @pl.loop(1, DAY)
    def _(off):
        pl.semaphore_signal(barrier, inc=1, device_id={"day": lax.rem(day + off, DAY)}, device_id_type=MESH)

    def tile_copy(src, dst, ssem, rsem, peer):
        return pltpu.make_async_remote_copy(
            src_ref=src, dst_ref=dst, send_sem=ssem, recv_sem=rsem,
            device_id={"tile": peer}, device_id_type=MESH,
        )

    def day_copy(src, dst, ssem, rsem, peer):
        return pltpu.make_async_remote_copy(
            src_ref=src, dst_ref=dst, send_sem=ssem, recv_sem=rsem,
            device_id={"day": peer}, device_id_type=MESH,
        )

    row = lax.broadcasted_iota(jnp.int32, (R, L), 0)
    column = lax.broadcasted_iota(jnp.int32, (R, L), 1)
    total = None
    for n in range(N):
        place = jnp.where(row + n * R == column, 1.0, 0.0).astype(BF16)
        factor = dot(clon[...], place).astype(BF16)
        part = dot(coarse[n], factor)
        total = part if total is None else total + part
    along[...] = total.reshape(C, A, L)
    for t in range(TR):
        acc = cvar[0, t] * along[0]
        for c in range(1, C):
            acc = acc + cvar[c, t] * along[c]
        wall[me, t] = acc
    wall[me, TR] = jnp.zeros((A, L), F32)
    wall[me, TR, :, 0:S] = clat[...].astype(F32)

    pl.semaphore_wait(barrier, T - 1 + DAY - 1)

    def w_copy(slot, off, peer):
        return tile_copy(wall.at[slot], wall.at[slot], s_w.at[off], r_w.at[off], peer)

    @pl.loop(1, T)
    def _(off):
        w_copy(me, off, lax.rem(me + off, T)).start()

    for n in range(N):
        place = jnp.where(row + n * R == column, 1.0, 0.0).astype(BF16)
        place_t = jnp.where(
            lax.broadcasted_iota(jnp.int32, (L, R), 1) + n * R
            == lax.broadcasted_iota(jnp.int32, (L, R), 0), 1.0, 0.0
        ).astype(BF16)

        @pl.loop(0, NB)
        def _(b):
            rows = pl.ds(pl.multiple_of(b * JB, JB), JB)
            block = flon[rows, :]
            lon_pad[n, rows, :] = dot(block, place).astype(BF16)
            lon_pad_t[n, b] = dot_nt(place_t, block).astype(BF16)

    back[...] = jnp.zeros_like(back)
    fva[...] = jnp.zeros_like(fva)
    xs[...] = jnp.zeros_like(xs)
    qsend[:, TR] = jnp.zeros((T, A, L), F32)
    if rr < 8:
        fsend[...] = jnp.zeros_like(fsend)

    @pl.loop(1, T)
    def _(off):
        w_copy(lax.rem(me - off + T, T), off, lax.rem(me + off, T)).wait_recv()

    for t in range(TR):
        wfl[:, t * L:(t + 1) * L] = wall[:, t].reshape(T * A, L)
    lat_all = wall[:, TR].reshape(T * A, L)
    lat_t = jnp.transpose(lat_all)[0:S].astype(BF16)
    core[...] = dot_exact(lat_t, wfl[...])
    mixed[...] = dot_exact(flat[...], core[...])

    CH = min(32, I)

    @pl.loop(0, I // CH)
    def _(q):
        rows = pl.ds(pl.multiple_of(q * CH, CH), CH)
        for v in range(V):
            acc = fvar[v, 0] * mixed[rows, 0:L]
            for t in range(1, TR):
                acc = acc + fvar[v, t] * mixed[rows, t * L:(t + 1) * L]
            lifted[v, rows, :] = acc.astype(BF16)

    for v in range(V):
        lifted_t[v] = jnp.transpose(lifted[v].astype(F32)).astype(BF16)

    def gd_send(k, off):
        to = lax.rem(day + off, DAY)
        return day_copy(
            gl.at[k, :, pl.ds(pl.multiple_of(to * rq, rq), rq), :], gday.at[k, day],
            s_gd.at[k, off], r_gd.at[k, off], to,
        )

    def gd_recv(k, off):
        source = lax.rem(day - off + DAY, DAY)
        return day_copy(
            gl.at[k, :, pl.ds(pl.multiple_of(day * rq, rq), rq), :], gday.at[k, source],
            s_gd.at[k, off], r_gd.at[k, off], source,
        )

    def gt_send(k, q, owner):
        off = lax.rem(owner - me + T, T)
        return tile_copy(gown.at[k, q], gtile.at[me], s_gt.at[off], r_gt.at[off], owner)

    def gt_recv(off):
        source = lax.rem(me - off + T, T)
        return tile_copy(gown.at[0, 0], gtile.at[source], s_gt.at[off], r_gt.at[off], source)

    def pass_on(k):
        for off in range(1, DAY):
            gd_recv(k, off).wait_recv()
        acc = gday[k, 0]
        for e in range(1, DAY):
            acc = acc + gday[k, e]
        gown[k] = acc
        for q in range(NSUB):
            owner = block_of(k) * NSUB + q

            @pl.when(owner != me)
            def _():
                gt_send(k, q, owner).start()

            @pl.when(owner == me)
            def _():
                gtile[me] = acc[q]

    @pl.loop(0, NB)
    def _(k):
        fine_copy(k).wait()
        b = block_of(k)
        rows = pl.ds(pl.multiple_of(b * JB, JB), JB)
        grad = None
        for v in range(V):
            term = None
            for n in range(N):
                predicted = dot(lifted[v], lon_pad_t[n, b])
                residual = (predicted - fbuf[k, n, v].astype(F32)).astype(BF16)
                part = dot(residual, lon_pad[n, rows, :])
                term = part if term is None else term + part
                piece = dot(lifted_t[v, n * R:(n + 1) * R, :], residual)
                grad = piece if grad is None else grad + piece
            back[v] += term
        for q in range(NSUB):
            gl[k, q] = grad[:, q * jb:(q + 1) * jb]
        gday[k, day] = gl[k, :, pl.ds(pl.multiple_of(day * rq, rq), rq), :]
        for off in range(1, DAY):
            gd_send(k, off).start()

        @pl.when(k >= 2)
        def _():
            pass_on(k - 2)

    @pl.loop(0, I // CH)
    def _(q):
        rows = pl.ds(pl.multiple_of(q * CH, CH), CH)
        for t in range(TR):
            acc = fvar[0, t] * back[0, rows, :]
            for v in range(1, V):
                acc = acc + fvar[v, t] * back[v, rows, :]
            spread[rows, t * L:(t + 1) * L] = acc

    scale = math.sqrt(S * R * TR / (I * T * J * V))
    flat_t = jnp.transpose(flat[...].astype(F32)).astype(BF16)
    core_grad = dot_exact(flat_t, spread[...]) * scale
    wanted = dot_exact(lat_all[:, 0:S].astype(BF16), core_grad)
    for t in range(TR):
        qsend[:, t] = wanted[:, t * L:(t + 1) * L].reshape(T, A, L)
    qsend[:, TR, :, 0:S] = dot_nt_three(wfl[...], core_grad).reshape(T, A, S)
    qrecv[me] = qsend[me]

    def q_send(off):
        peer = lax.rem(me + off, T)
        return tile_copy(qsend.at[peer], qrecv.at[me], s_q.at[off], r_q.at[off], peer)

    def q_recv(off):
        source = lax.rem(me - off + T, T)
        return tile_copy(qsend.at[me], qrecv.at[source], s_q.at[off], r_q.at[off], source)

    @pl.loop(1, T)
    def _(off):
        q_send(off).start()

    for k in range(max(NB - 2, 0), NB):
        pass_on(k)

    lat_day[day] = dot_nt_three(spread[...], core[...])

    def own_send(buf, ssem, rsem, off):
        return day_copy(buf.at[day], buf.at[day], ssem.at[off], rsem.at[off], lax.rem(day + off, DAY))

    def own_recv(buf, ssem, rsem, off):
        source = lax.rem(day - off + DAY, DAY)
        return day_copy(buf.at[source], buf.at[source], ssem.at[off], rsem.at[off], source)

    for off in range(1, DAY):
        own_send(lat_day, s_ld, r_ld, off).start()

    @pl.loop(0, I // CH)
    def _(q):
        rows = pl.ds(pl.multiple_of(q * CH, CH), CH)
        for v in range(V):
            held = back[v, rows, :]
            for t in range(TR):
                product = held * mixed[rows, t * L:(t + 1) * L]
                fva[v * TR + t] += jnp.sum(product.reshape(CH // 8, 8, L), axis=0)

    xs[C * TR:C * TR + V * TR, :] = jnp.sum(fva[...], axis=1)

    @pl.loop(1, T)
    def _(off):
        q_recv(off).wait_recv()

    summed = qrecv[0]
    for p in range(1, T):
        summed = summed + qrecv[p]
    clat_day[day] = summed[TR]
    for off in range(1, DAY):
        own_send(clat_day, s_cd, r_cd, off).start()
    q_of = summed[0:TR]
    for c in range(C):
        acc = cvar[c, 0] * q_of[0]
        for t in range(1, TR):
            acc = acc + cvar[c, t] * q_of[t]
        vv[c * A:(c + 1) * A, :] = acc
        xs[c * TR:(c + 1) * TR, :] = jnp.sum(along[c][None] * q_of, axis=1)
    v_high, v_low = halves(jnp.transpose(vv[...]))
    lon_t = None
    for n in range(N):
        mine = slice(n * R, (n + 1) * R)
        part = dot(v_high[mine], coarse[n]) + dot(v_low[mine], coarse[n])
        lon_t = part if lon_t is None else lon_t + part
    x_high, x_low = halves(xs[...])
    ones = jnp.ones((8, L), BF16)
    small = dot_nt(ones, x_high) + dot_nt(ones, x_low)
    B = lon_t.shape[1]
    for p in range(T):
        fsend[p, 0, 0:rr, :] = lon_t[p * rr:(p + 1) * rr, :]
        fsend[p, 1] = small
    frecv[me] = fsend[me]

    def f_send(off):
        peer = lax.rem(me + off, T)
        return tile_copy(fsend.at[peer], frecv.at[me], s_fs.at[off], r_fs.at[off], peer)

    def f_recv(off):
        source = lax.rem(me - off + T, T)
        return tile_copy(fsend.at[me], frecv.at[source], s_fs.at[off], r_fs.at[off], source)

    @pl.loop(1, T)
    def _(off):
        f_send(off).start()

    @pl.loop(1, T)
    def _(off):
        gt_recv(off).wait_recv()

    rows_sum = gtile[0]
    for p in range(1, T):
        rows_sum = rows_sum + gtile[p]
    gfin[day] = rows_sum
    for off in range(1, DAY):
        own_send(gfin, s_gf, r_gf, off).start()

    @pl.loop(1, T)
    def _(off):
        f_recv(off).wait_recv()

    fsum = frecv[0]
    for p in range(1, T):
        fsum = fsum + frecv[p]
    fday[day] = fsum
    for off in range(1, DAY):
        own_send(fday, s_fd, r_fd, off).start()

    days = N * DAY
    for off in range(1, DAY):
        own_recv(lat_day, s_ld, r_ld, off).wait_recv()
    acc = lat_day[0]
    for e in range(1, DAY):
        acc = acc + lat_day[e]
    o_flat[...] = acc * (1.0 / math.sqrt(days * V * J))
    for off in range(1, DAY):
        own_recv(clat_day, s_cd, r_cd, off).wait_recv()
    acc = clat_day[0]
    for e in range(1, DAY):
        acc = acc + clat_day[e]
    o_clat[...] = acc * (1.0 / math.sqrt(days * R * TR))

    for off in range(1, DAY):
        own_recv(fday, s_fd, r_fd, off).wait_recv()
    ftotal = fday[0]
    for e in range(1, DAY):
        ftotal = ftotal + fday[e]
    fall[me] = ftotal[0]

    def a_copy(slot, off, peer):
        return tile_copy(fall.at[slot], fall.at[slot], s_fa.at[off], r_fa.at[off], peer)

    @pl.loop(1, T)
    def _(off):
        a_copy(me, off, lax.rem(me + off, T)).start()

    o_small[...] = ftotal[1]
    for off in range(1, DAY):
        own_recv(gfin, s_gf, r_gf, off).wait_recv()
    o_flon[...] = gfin[...] * (1.0 / math.sqrt(days * V * I * T))

    @pl.loop(1, T)
    def _(off):
        a_copy(lax.rem(me - off + T, T), off, lax.rem(me + off, T)).wait_recv()

    o_fin[...] = fall[...] * (1.0 / math.sqrt(days * S * TR))

    @pl.loop(1, T)
    def _(off):
        w_copy(me, off, lax.rem(me + off, T)).wait_send()
        q_send(off).wait_send()
        gt_recv(off).wait_send()
        f_send(off).wait_send()
        a_copy(me, off, lax.rem(me + off, T)).wait_send()

    for off in range(1, DAY):
        own_send(lat_day, s_ld, r_ld, off).wait_send()
        own_send(clat_day, s_cd, r_cd, off).wait_send()
        own_send(gfin, s_gf, r_gf, off).wait_send()
        own_send(fday, s_fd, r_fd, off).wait_send()

        @pl.loop(0, NB)
        def _(k):
            gd_send(k, off).wait_send()


def per_device(T, DAY, coarse, fine, coarse_lat, coarse_lon, coarse_var, fine_lat, fine_lon, fine_var):
    N, C, a_own, B = coarse.shape
    A = -(-a_own // 8) * 8
    if A != a_own:
        coarse = jnp.pad(coarse, ((0, 0), (0, 0), (0, A - a_own), (0, 0)))
        coarse_lat = jnp.pad(coarse_lat, ((0, A - a_own), (0, 0)))
    R, S, TR = coarse_lon.shape[1], coarse_lat.shape[1], coarse_var.shape[1]
    V, I, J = fine.shape[1], fine.shape[2], fine.shape[3]
    jb = J // T
    JB = max(512, jb)
    NB, NSUB = J // JB, JB // jb
    rq, rr = R // DAY, R // T
    RP = max(rr, 8)
    L = N * R
    W = TR * L
    XS = -(-(C * TR + V * TR) // LANES) * LANES
    XS = max(XS, B)
    d = dict(T=T, DAY=DAY, N=N, C=C, A=A, R=R, S=S, TR=TR, V=V, I=I, J=J,
             JB=JB, NB=NB, NSUB=NSUB, jb=jb, rq=rq, rr=rr)
    vmem = pl.BlockSpec(memory_space=pltpu.VMEM)
    smem = pl.BlockSpec(memory_space=pltpu.SMEM)
    dma = lambda *shape: pltpu.SemaphoreType.DMA(shape)
    buf = lambda *shape: pltpu.VMEM(shape, F32)
    half = lambda *shape: pltpu.VMEM(shape, BF16)
    o_flat, o_flon, o_fin, o_small, o_clat = pl.pallas_call(
        functools.partial(kernel, d),
        out_shape=(
            jax.ShapeDtypeStruct((I, S), F32),
            jax.ShapeDtypeStruct((DAY, rq, jb), F32),
            jax.ShapeDtypeStruct((T, RP, B), F32),
            jax.ShapeDtypeStruct((8, XS), F32),
            jax.ShapeDtypeStruct((A, L), F32),
        ),
        in_specs=[smem, smem, vmem, vmem, vmem, vmem, vmem, pl.BlockSpec(memory_space=pl.ANY)],
        out_specs=(vmem,) * 5,
        scratch_shapes=[
            half(NB, N, V, I, JB), buf(C, A, L), buf(T, TR + 1, A, L), buf(T * A, W), buf(S, W),
            buf(I, W), half(V, I, L), half(V, L, I), half(N, J, L), half(N, NB, L, JB),
            buf(V, I, L), buf(I, W), buf(V * TR, 8, L), buf(NB, NSUB, R, jb),
            buf(NB, DAY, NSUB, rq, jb), buf(NB, NSUB, rq, jb), buf(T, rq, jb), buf(DAY, rq, jb),
            buf(T, TR + 1, A, L), buf(T, TR + 1, A, L), buf(C * A, L), buf(XS, L),
            buf(DAY, I, S), buf(DAY, A, L), buf(T, 2, RP, B), buf(T, 2, RP, B),
            buf(DAY, 2, RP, B), buf(T, RP, B),
            dma(NB), dma(T), dma(T), dma(T), dma(T), dma(NB, DAY), dma(NB, DAY), dma(T), dma(T),
            dma(DAY), dma(DAY), dma(DAY), dma(DAY), dma(DAY), dma(DAY), dma(T), dma(T),
            dma(DAY), dma(DAY), dma(T), dma(T),
        ],
        compiler_params=pltpu.CompilerParams(
            collective_id=0, has_side_effects=True, vmem_limit_bytes=60 * 1024 * 1024
        ),
    )(
        coarse_var.astype(F32), fine_var.astype(F32), coarse.reshape(N, C * A, B), coarse_lat,
        coarse_lon, fine_lat, fine_lon, fine,
    )
    days = N * DAY
    small = o_small[0]
    return (
        o_flat,
        o_flon.reshape(R, jb).T,
        small[C * TR:C * TR + V * TR].reshape(V, TR) / math.sqrt(days * I * T * J),
        o_clat[:a_own, :S],
        o_fin[:, :rr].reshape(R, B).T,
        small[:C * TR].reshape(C, TR) / math.sqrt(days * S * R),
    )


def solution(mesh):
    in_specs = (
        P("day", None, "tile", None),
        P("day", None, "tile", None),
        P("tile", None),
        P(),
        P(),
        P("tile", None),
        P(),
        P(),
    )
    out_specs = (P("tile", None), P("tile", None), P(), P("tile", None), P(), P())
    return jax.shard_map(
        functools.partial(per_device, mesh.shape["tile"], mesh.shape["day"]),
        mesh=mesh, in_specs=in_specs, out_specs=out_specs, check_vma=False,
    )
```

time: 434 us -> 89.3 us (0.21)
  waiting for transfers between devices: 284 us -> 0 us
  Pallas kernels: 0 us -> 71.3 us
  matrix products: 65.5 us -> 0 us
  blocking collectives: 45.9 us -> 0 us
  between operations: 13.9 us -> 0.65 us
  other arithmetic: 8.16 us -> 2.73 us
    psum x4 -> x0, waiting for transfers between devices: 284 us -> none  [the longest x1 123 us: per_device(): lax.psum((grad_second_coarse, grad_third_coarse, grad_var_fine), ('tile',...]
    pallas_call x0 -> x1, Pallas kernels: none -> 71.3 us  [per_device(): pl.pallas_call(functools.partial(kernel, d), out_shape=(jax.ShapeDtypeStr...]
    dot_general x19 -> x0, matrix products: 65.5 us -> none  [the longest x1 11.8 us: per_device(): jnp.dot(residual, fine_lon, preferred_element_type=jnp.float32)]
    psum x2 -> x0, blocking collectives: 45.9 us -> none  [the longest x1 40 us: per_device(): lax.psum((grad_second_coarse, grad_third_coarse, grad_var_fine), ('tile',...]
    unnamed x14 -> x8, local copies, waits for them, and re-layouts: 1.68 us -> 12 us
    div x6 -> x2, other arithmetic: 6.29 us -> 1.47 us  [the longest x1 0.76 us: per_device(): small[C * TR:C * TR + V * TR].reshape(V, TR) / math.sqrt(days * I * T * J)]
    dot_general x2 -> x0, local copies, waits for them, and re-layouts: 4.66 us -> none  [the longest x1 2.87 us: per_device(): jnp.einsum('ct,nsrt->ncsr', var_float, core_grad, precision=HIGHEST)]
  transfers between devices with their start and end apart: 5 -> 0, of which waited for: 4 -> 0; matrix products, arithmetic and copies ran while one was open for 10% -> 0% of each run, Pallas kernels for 0% -> 0%
where the time goes in v1:
time: 89.3 us; the launch traced here: 88.7 us
  Pallas kernels  71.3 us (80%)
  local copies, waits for them, and re-layouts  14.1 us (16%)
  other arithmetic  2.73 us (3%)
    pallas_call x1, Pallas kernels, per_device(): pl.pallas_call(functools.partial(kernel, d), out_shape=(jax.ShapeDtypeStr...  71.3 us
    unnamed x8, local copies, waits for them, and re-layouts  12 us

profile of v1, /device:TPU:0, one launch (start us, length us, event | category | flops | bytes accessed | tf_op | source)
XLA Modules:
  0.0 88.7 jit_solution(1287340841949172980)
XLA Ops:
  0.6 1.3 %convert_element_type.7.fvar = f32[4,8]{1,0:T(4,128)} convert(bf16[4,8]{1,0:T(4,128)(2,1)} %param.15) | non-fusion elementwise | flops 32 | bytes 192 | tf_op jit(solution)/shard_map/convert_element_type | solution.py:462
  1.9 1.4 %copy.26.cvar = f32[20,8]{1,0:T(8,128)} copy(bf16[20,8]{0,1:T(8,128)(2,1)} %param.12) | data formatting | bytes 960 | tf_op jit(solution)/shard_map/convert_element_type | solution.py:462
  3.2 1.5 %copy.27.clon = bf16[256,64]{1,0:T(8,128)(2,1)} copy(bf16[256,64]{0,1:T(8,128)(2,1)} %param.11) | data formatting | bytes 65536 | tf_op args[3]
  4.7 1.5 %copy.28.flat = bf16[256,64]{1,0:T(8,128)(2,1)} copy(bf16[256,64]{0,1:T(8,128)(2,1)} %param.13) | data formatting | bytes 65536 | tf_op args[5]
  6.2 2.4 %copy.29.flon = bf16[4096,64]{1,0:T(8,128)(2,1)} copy(bf16[4096,64]{0,1:T(8,128)(2,1)} %param.14) | data formatting | bytes 1048576 | tf_op args[6]
  8.6 71.3 %shard_map.127 = (f32[256,64]{1,0:T(8,128)}, f32[4,16,512]{2,1,0:T(8,128)}, f32[8,8,256]{2,1,0:T(8,128)}, f32[8,256]{1,0:T(8,128)}, f32[16,128]{1,0:T(8,128)}) custom-call(f32[20,8]{1,0:T(8,128)} %copy.26.cvar, f32[4,8]{1,0:T(4,128)} %convert_element_type.7.fvar, bf16[2,320,256]{2,1,0:T(8,128)(2,1)} %bitcast.8, bf16[16,64]{1,0:T(8,128)(2,1)} %clat.1, ...), custom_call_target="tpu_custom_call" | custom-call | tf_op jit(solution)/shard_map/pallas_call | solution.py:435
  79.9 1.6 %copy.30 = f32[256,64]{0,1:T(8,128)} copy(f32[256,64]{1,0:T(8,128)} %get-tuple-element.28) | data formatting | bytes 131072
  81.5 0.8 multiply_reduce_fusion.1
  82.3 0.7 multiply_reduce_fusion
  83.0 0.7 div.18
  83.6 0.1 div.21
  83.7 0.7 copy.31
  84.4 1.6 %copy.35 = f32[512,64]{0,1:T(8,128)} copy(f32[512,64]{0,1:T(8,128)} %bitcast.9) | data formatting | bytes 262144
  86.0 1.3 %copy.36 = f32[16,64]{1,0:T(8,128)} copy(f32[16,64]{1,0:T(8,128)} %bitcast.11) | data formatting | bytes 8192
  87.3 1.5 %copy.37 = f32[256,64]{0,1:T(8,128)} copy(f32[256,64]{0,1:T(8,128)} %bitcast.10) | data formatting | bytes 131072

commit v2 on v1

--- a/solution.py
+++ b/solution.py
@@ -44,9 +44,9 @@
     o_flat, o_flon, o_fin, o_small, o_clat,
     fbuf, along, wall, wfl, core, mixed, lifted, lifted_t, lon_pad, lon_pad_t,
     back, spread, fva, gl, gday, gown, gtile, gfin,
-    qsend, qrecv, vv, xs, lat_day, clat_day, fsend, frecv, fday, fall,
+    qsend, qpart, qrecv, vv, xs, lat_day, clat_day, fsend, frecv, fday, fall,
     s_fine, s_w, r_w, s_q, r_q, s_gd, r_gd, s_gt, r_gt, s_gf, r_gf,
-    s_ld, r_ld, s_cd, r_cd, s_fs, r_fs, s_fd, r_fd, s_fa, r_fa,
+    s_ld, r_ld, s_cd, r_cd, s_fs, r_fs, s_fd, r_fd, s_fa, r_fa, s_x, r_x, s_y, r_y,
 ):
     T, DAY, N, C, A, R, S, TR, V, I, J = (
         d["T"], d["DAY"], d["N"], d["C"], d["A"], d["R"], d["S"], d["TR"], d["V"], d["I"], d["J"]
@@ -92,43 +92,67 @@
 
     row = lax.broadcasted_iota(jnp.int32, (R, L), 0)
     column = lax.broadcasted_iota(jnp.int32, (R, L), 1)
+    row_t = lax.broadcasted_iota(jnp.int32, (L, R), 0)
+    column_t = lax.broadcasted_iota(jnp.int32, (L, R), 1)
     total = None
     for n in range(N):
-        place = jnp.where(row + n * R == column, 1.0, 0.0).astype(BF16)
-        factor = dot(clon[...], place).astype(BF16)
-        part = dot(coarse[n], factor)
+        place_t = jnp.where(column_t + n * R == row_t, 1.0, 0.0).astype(BF16)
+        factor_t = dot(place_t, clon[...]).astype(BF16)
+        part = dot_nt(coarse[n], factor_t)
         total = part if total is None else total + part
     along[...] = total.reshape(C, A, L)
     for t in range(TR):
-        acc = cvar[0, t] * along[0]
+        acc = cvar[t, 0] * along[0]
         for c in range(1, C):
-            acc = acc + cvar[c, t] * along[c]
+            acc = acc + cvar[t, c] * along[c]
         wall[me, t] = acc
     wall[me, TR] = jnp.zeros((A, L), F32)
     wall[me, TR, :, 0:S] = clat[...].astype(F32)
 
     pl.semaphore_wait(barrier, T - 1 + DAY - 1)
 
-    def w_copy(slot, off, peer):
-        return tile_copy(wall.at[slot], wall.at[slot], s_w.at[off], r_w.at[off], peer)
-
-    @pl.loop(1, T)
-    def _(off):
-        w_copy(me, off, lax.rem(me + off, T)).start()
+    H = T // 2
+    pair, member = lax.div(me, 2), lax.rem(me, 2)
+    partner = pair * 2 + 1 - member
+
+    def ahead(off):
+        return lax.rem(pair + off, H)
+
+    def behind(off):
+        return lax.rem(pair - off + H, H)
+
+    def w_along(off):
+        return tile_copy(wall.at[me], wall.at[me], s_w.at[off], r_w.at[off], ahead(off) * 2 + member)
+
+    def w_along_in(off):
+        slot = behind(off) * 2 + member
+        return tile_copy(wall.at[slot], wall.at[slot], s_w.at[off], r_w.at[off], slot)
+
+    def w_across(off):
+        slot = behind(off) * 2 + member
+        return tile_copy(wall.at[slot], wall.at[slot], s_x.at[off], r_x.at[off], partner)
+
+    def w_across_in(off):
+        slot = behind(off) * 2 + 1 - member
+        return tile_copy(wall.at[slot], wall.at[slot], s_x.at[off], r_x.at[off], partner)
+
+    @pl.loop(1, H)
+    def _(off):
+        w_along(off).start()
+
+    w_across(0).start()
 
     for n in range(N):
         place = jnp.where(row + n * R == column, 1.0, 0.0).astype(BF16)
-        place_t = jnp.where(
-            lax.broadcasted_iota(jnp.int32, (L, R), 1) + n * R
-            == lax.broadcasted_iota(jnp.int32, (L, R), 0), 1.0, 0.0
-        ).astype(BF16)
+        place_t = jnp.where(column_t + n * R == row_t, 1.0, 0.0).astype(BF16)
 
         @pl.loop(0, NB)
         def _(b):
             rows = pl.ds(pl.multiple_of(b * JB, JB), JB)
-            block = flon[rows, :]
+            block_t = flon[:, rows]
+            block = jnp.transpose(block_t.astype(F32)).astype(BF16)
             lon_pad[n, rows, :] = dot(block, place).astype(BF16)
-            lon_pad_t[n, b] = dot_nt(place_t, block).astype(BF16)
+            lon_pad_t[n, b] = dot(place_t, block_t).astype(BF16)
 
     back[...] = jnp.zeros_like(back)
     fva[...] = jnp.zeros_like(fva)
@@ -137,16 +161,21 @@
     if rr < 8:
         fsend[...] = jnp.zeros_like(fsend)
 
-    @pl.loop(1, T)
-    def _(off):
-        w_copy(lax.rem(me - off + T, T), off, lax.rem(me + off, T)).wait_recv()
+    @pl.loop(1, H)
+    def _(off):
+        w_along_in(off).wait_recv()
+        w_across(off).start()
+
+    @pl.loop(0, H)
+    def _(off):
+        w_across_in(off).wait_recv()
 
     for t in range(TR):
         wfl[:, t * L:(t + 1) * L] = wall[:, t].reshape(T * A, L)
     lat_all = wall[:, TR].reshape(T * A, L)
     lat_t = jnp.transpose(lat_all)[0:S].astype(BF16)
     core[...] = dot_exact(lat_t, wfl[...])
-    mixed[...] = dot_exact(flat[...], core[...])
+    mixed[...] = dot_exact(jnp.transpose(flat[...].astype(F32)).astype(BF16), core[...])
 
     CH = min(32, I)
 
@@ -238,30 +267,47 @@
             spread[rows, t * L:(t + 1) * L] = acc
 
     scale = math.sqrt(S * R * TR / (I * T * J * V))
-    flat_t = jnp.transpose(flat[...].astype(F32)).astype(BF16)
-    core_grad = dot_exact(flat_t, spread[...]) * scale
+    core_grad = dot_exact(flat[...], spread[...]) * scale
     wanted = dot_exact(lat_all[:, 0:S].astype(BF16), core_grad)
     for t in range(TR):
         qsend[:, t] = wanted[:, t * L:(t + 1) * L].reshape(T, A, L)
     qsend[:, TR, :, 0:S] = dot_nt_three(wfl[...], core_grad).reshape(T, A, S)
-    qrecv[me] = qsend[me]
+
+    def q_across(off):
+        slot = ahead(off) * 2 + 1 - member
+        return tile_copy(qsend.at[slot], qpart.at[ahead(off)], s_y.at[off], r_y.at[off], partner)
 
     def q_send(off):
-        peer = lax.rem(me + off, T)
-        return tile_copy(qsend.at[peer], qrecv.at[me], s_q.at[off], r_q.at[off], peer)
+        return tile_copy(
+            qpart.at[ahead(off)], qrecv.at[pair], s_q.at[off], r_q.at[off], ahead(off) * 2 + member
+        )
 
     def q_recv(off):
-        source = lax.rem(me - off + T, T)
-        return tile_copy(qsend.at[me], qrecv.at[source], s_q.at[off], r_q.at[off], source)
-
-    @pl.loop(1, T)
-    def _(off):
+        source = behind(off)
+        return tile_copy(
+            qpart.at[pair], qrecv.at[source], s_q.at[off], r_q.at[off], source * 2 + member
+        )
+
+    @pl.loop(1, H)
+    def _(off):
+        q_across(off).start()
+
+    q_across(0).start()
+
+    lat_day[day] = dot_nt_three(core[...], spread[...])
+
+    @pl.loop(1, H)
+    def _(off):
+        q_across(off).wait_recv()
+        slot = ahead(off)
+        qpart[slot] = qpart[slot] + qsend[slot * 2 + member]
         q_send(off).start()
+
+    q_across(0).wait_recv()
+    qrecv[pair] = qpart[pair] + qsend[me]
 
     for k in range(max(NB - 2, 0), NB):
         pass_on(k)
-
-    lat_day[day] = dot_nt_three(spread[...], core[...])
 
     def own_send(buf, ssem, rsem, off):
         return day_copy(buf.at[day], buf.at[day], ssem.at[off], rsem.at[off], lax.rem(day + off, DAY))
@@ -284,21 +330,21 @@
 
     xs[C * TR:C * TR + V * TR, :] = jnp.sum(fva[...], axis=1)
 
-    @pl.loop(1, T)
+    @pl.loop(1, H)
     def _(off):
         q_recv(off).wait_recv()
 
     summed = qrecv[0]
-    for p in range(1, T):
+    for p in range(1, H):
         summed = summed + qrecv[p]
     clat_day[day] = summed[TR]
     for off in range(1, DAY):
         own_send(clat_day, s_cd, r_cd, off).start()
     q_of = summed[0:TR]
     for c in range(C):
-        acc = cvar[c, 0] * q_of[0]
+        acc = cvar[0, c] * q_of[0]
         for t in range(1, TR):
-            acc = acc + cvar[c, t] * q_of[t]
+            acc = acc + cvar[t, c] * q_of[t]
         vv[c * A:(c + 1) * A, :] = acc
         xs[c * TR:(c + 1) * TR, :] = jnp.sum(along[c][None] * q_of, axis=1)
     v_high, v_low = halves(jnp.transpose(vv[...]))
@@ -308,7 +354,7 @@
         part = dot(v_high[mine], coarse[n]) + dot(v_low[mine], coarse[n])
         lon_t = part if lon_t is None else lon_t + part
     x_high, x_low = halves(xs[...])
-    ones = jnp.ones((8, L), BF16)
+    ones = jnp.ones((d["RP"], L), BF16)
     small = dot_nt(ones, x_high) + dot_nt(ones, x_low)
     B = lon_t.shape[1]
     for p in range(T):
@@ -350,19 +396,18 @@
     for off in range(1, DAY):
         own_send(fday, s_fd, r_fd, off).start()
 
-    days = N * DAY
     for off in range(1, DAY):
         own_recv(lat_day, s_ld, r_ld, off).wait_recv()
     acc = lat_day[0]
     for e in range(1, DAY):
         acc = acc + lat_day[e]
-    o_flat[...] = acc * (1.0 / math.sqrt(days * V * J))
+    o_flat[...] = acc
     for off in range(1, DAY):
         own_recv(clat_day, s_cd, r_cd, off).wait_recv()
     acc = clat_day[0]
     for e in range(1, DAY):
         acc = acc + clat_day[e]
-    o_clat[...] = acc * (1.0 / math.sqrt(days * R * TR))
+    o_clat[...] = acc
 
     for off in range(1, DAY):
         own_recv(fday, s_fd, r_fd, off).wait_recv()
@@ -381,21 +426,29 @@
     o_small[...] = ftotal[1]
     for off in range(1, DAY):
         own_recv(gfin, s_gf, r_gf, off).wait_recv()
-    o_flon[...] = gfin[...] * (1.0 / math.sqrt(days * V * I * T))
+    o_flon[...] = gfin[...]
 
     @pl.loop(1, T)
     def _(off):
         a_copy(lax.rem(me - off + T, T), off, lax.rem(me + off, T)).wait_recv()
 
-    o_fin[...] = fall[...] * (1.0 / math.sqrt(days * S * TR))
-
-    @pl.loop(1, T)
-    def _(off):
-        w_copy(me, off, lax.rem(me + off, T)).wait_send()
-        q_send(off).wait_send()
+    o_fin[...] = fall[...]
+
+    @pl.loop(1, T)
+    def _(off):
         gt_recv(off).wait_send()
         f_send(off).wait_send()
         a_copy(me, off, lax.rem(me + off, T)).wait_send()
+
+    @pl.loop(1, H)
+    def _(off):
+        w_along(off).wait_send()
+        q_send(off).wait_send()
+
+    @pl.loop(0, H)
+    def _(off):
+        w_across(off).wait_send()
+        q_across(off).wait_send()
 
     for off in range(1, DAY):
         own_send(lat_day, s_ld, r_ld, off).wait_send()
@@ -406,6 +459,36 @@
         @pl.loop(0, NB)
         def _(k):
             gd_send(k, off).wait_send()
+
+
+def finish(d, days, flat, flon, fin, small, clat, o_flat, o_flon, o_fvar, o_clat, o_clon, o_cvar):
+    T, DAY, C, R, S, TR, V, I, J = (
+        d["T"], d["DAY"], d["C"], d["R"], d["S"], d["TR"], d["V"], d["I"], d["J"]
+    )
+    rq, rr = d["rq"], d["rr"]
+    o_flat[...] = flat[...] * (1.0 / math.sqrt(days * V * J))
+    for e in range(DAY):
+        o_flon[e * rq:(e + 1) * rq, :] = flon[e] * (1.0 / math.sqrt(days * V * I * T))
+    for p in range(T):
+        o_clon[p * rr:(p + 1) * rr, :] = fin[p, 0:rr] * (1.0 / math.sqrt(days * S * TR))
+    own = o_clat.shape[0]
+    o_clat[...] = clat[0:own, 0:S] * (1.0 / math.sqrt(days * R * TR))
+    width = small.shape[1]
+    line = jnp.broadcast_to(small[0:1, :], (8, width))
+    row = lax.broadcasted_iota(jnp.int32, (8, width), 0)
+    lane = lax.broadcasted_iota(jnp.int32, (8, width), 1)
+    at = lax.broadcasted_iota(jnp.int32, (LANES, width), 1)
+    to = lax.broadcasted_iota(jnp.int32, (LANES, width), 0)
+
+    def placed(kept, chosen):
+        high, low = halves(jnp.where(kept, line, 0.0))
+        chosen = jnp.where(chosen, 1.0, 0.0).astype(BF16)
+        return dot_nt(high, chosen) + dot_nt(low, chosen)
+
+    by_variable = placed(lax.rem(lane, TR) == row, lax.div(at, TR) == to)
+    o_cvar[...] = by_variable[0:TR, 0:C] * (1.0 / math.sqrt(days * S * R))
+    by_fine = placed(lax.div(lane, TR) == row + C, lax.rem(at, TR) == to)
+    o_fvar[...] = by_fine[0:V, 0:TR] * (1.0 / math.sqrt(days * I * T * J))
 
 
 def per_device(T, DAY, coarse, fine, coarse_lat, coarse_lon, coarse_var, fine_lat, fine_lon, fine_var):
@@ -426,7 +509,7 @@
     XS = -(-(C * TR + V * TR) // LANES) * LANES
     XS = max(XS, B)
     d = dict(T=T, DAY=DAY, N=N, C=C, A=A, R=R, S=S, TR=TR, V=V, I=I, J=J,
-             JB=JB, NB=NB, NSUB=NSUB, jb=jb, rq=rq, rr=rr)
+             JB=JB, NB=NB, NSUB=NSUB, jb=jb, rq=rq, rr=rr, RP=RP)
     vmem = pl.BlockSpec(memory_space=pltpu.VMEM)
     smem = pl.BlockSpec(memory_space=pltpu.SMEM)
     dma = lambda *shape: pltpu.SemaphoreType.DMA(shape)
@@ -435,10 +518,10 @@
     o_flat, o_flon, o_fin, o_small, o_clat = pl.pallas_call(
         functools.partial(kernel, d),
         out_shape=(
-            jax.ShapeDtypeStruct((I, S), F32),
+            jax.ShapeDtypeStruct((S, I), F32),
             jax.ShapeDtypeStruct((DAY, rq, jb), F32),
             jax.ShapeDtypeStruct((T, RP, B), F32),
-            jax.ShapeDtypeStruct((8, XS), F32),
+            jax.ShapeDtypeStruct((RP, XS), F32),
             jax.ShapeDtypeStruct((A, L), F32),
         ),
         in_specs=[smem, smem, vmem, vmem, vmem, vmem, vmem, pl.BlockSpec(memory_space=pl.ANY)],
@@ -448,30 +531,35 @@
             buf(I, W), half(V, I, L), half(V, L, I), half(N, J, L), half(N, NB, L, JB),
             buf(V, I, L), buf(I, W), buf(V * TR, 8, L), buf(NB, NSUB, R, jb),
             buf(NB, DAY, NSUB, rq, jb), buf(NB, NSUB, rq, jb), buf(T, rq, jb), buf(DAY, rq, jb),
-            buf(T, TR + 1, A, L), buf(T, TR + 1, A, L), buf(C * A, L), buf(XS, L),
-            buf(DAY, I, S), buf(DAY, A, L), buf(T, 2, RP, B), buf(T, 2, RP, B),
+            buf(T, TR + 1, A, L), buf(T // 2, TR + 1, A, L), buf(T // 2, TR + 1, A, L), buf(C * A, L), buf(XS, L),
+            buf(DAY, S, I), buf(DAY, A, L), buf(T, 2, RP, B), buf(T, 2, RP, B),
             buf(DAY, 2, RP, B), buf(T, RP, B),
             dma(NB), dma(T), dma(T), dma(T), dma(T), dma(NB, DAY), dma(NB, DAY), dma(T), dma(T),
             dma(DAY), dma(DAY), dma(DAY), dma(DAY), dma(DAY), dma(DAY), dma(T), dma(T),
-            dma(DAY), dma(DAY), dma(T), dma(T),
+            dma(DAY), dma(DAY), dma(T), dma(T), dma(T), dma(T), dma(T), dma(T),
         ],
         compiler_params=pltpu.CompilerParams(
             collective_id=0, has_side_effects=True, vmem_limit_bytes=60 * 1024 * 1024
         ),
     )(
-        coarse_var.astype(F32), fine_var.astype(F32), coarse.reshape(N, C * A, B), coarse_lat,
-        coarse_lon, fine_lat, fine_lon, fine,
+        coarse_var.T.astype(F32), fine_var.astype(F32), coarse.reshape(N, C * A, B), coarse_lat,
+        coarse_lon.T, fine_lat.T, fine_lon.T, fine,
     )
     days = N * DAY
-    small = o_small[0]
-    return (
-        o_flat,
-        o_flon.reshape(R, jb).T,
-        small[C * TR:C * TR + V * TR].reshape(V, TR) / math.sqrt(days * I * T * J),
-        o_clat[:a_own, :S],
-        o_fin[:, :rr].reshape(R, B).T,
-        small[:C * TR].reshape(C, TR) / math.sqrt(days * S * R),
-    )
+    flat_t, flon_t, fvar, clat, clon_t, cvar_t = pl.pallas_call(
+        functools.partial(finish, d, days),
+        out_shape=(
+            jax.ShapeDtypeStruct((S, I), F32),
+            jax.ShapeDtypeStruct((R, jb), F32),
+            jax.ShapeDtypeStruct((V, TR), F32),
+            jax.ShapeDtypeStruct((a_own, S), F32),
+            jax.ShapeDtypeStruct((R, B), F32),
+            jax.ShapeDtypeStruct((TR, C), F32),
+        ),
+        in_specs=[vmem] * 5,
+        out_specs=(vmem,) * 6,
+    )(o_flat, o_flon, o_fin, o_small, o_clat)
+    return (flat_t.T, flon_t.T, fvar, clat, clon_t.T, cvar_t.T)
 
 
 def solution(mesh):

time: 89.3 us -> 70 us (0.78)
  local copies, waits for them, and re-layouts: 14.1 us -> 0 us
  Pallas kernels: 71.3 us -> 66.6 us
    unnamed x8 -> x0, local copies, waits for them, and re-layouts: 12 us -> none
    pallas_call x1, Pallas kernels: 71.3 us -> 65 us  [per_device(): pl.pallas_call(functools.partial(kernel, d), out_shape=(jax.ShapeDtypeStr...]
    pallas_call x0 -> x1, Pallas kernels: none -> 1.69 us  [per_device(): pl.pallas_call(functools.partial(finish, d, days), out_shape=(jax.ShapeDt...]
    div x2 -> x0, other arithmetic: 1.47 us -> none  [the longest x1 0.76 us: per_device(): small[C * TR:C * TR + V * TR].reshape(V, TR) / math.sqrt(days * I * T * J)]
    convert_element_type x1 -> x0, local copies, waits for them, and re-layouts: 1.36 us -> none  [per_device(): coarse_var.astype(F32)]
    convert_element_type x0 -> x1, other arithmetic: none -> 1.27 us  [per_device(): coarse_var.T.astype(F32)]
where the time goes in v2:
time: 70 us; the launch traced here: 69.8 us
  Pallas kernels  66.6 us (95%)
  other arithmetic  2.53 us (4%)
    pallas_call x1, Pallas kernels, per_device(): pl.pallas_call(functools.partial(kernel, d), out_shape=(jax.ShapeDtypeStr...  65 us
    pallas_call x1, Pallas kernels, per_device(): pl.pallas_call(functools.partial(finish, d, days), out_shape=(jax.ShapeDt...  1.69 us

profile of v2, /device:TPU:0, one launch (start us, length us, event | category | flops | bytes accessed | tf_op | source)
XLA Modules:
  0.0 69.8 jit_solution(1812762212417753277)
XLA Ops:
  0.6 1.3 %convert_element_type.10.fvar = f32[4,8]{1,0:T(4,128)} convert(bf16[4,8]{1,0:T(4,128)(2,1)} %param.15) | non-fusion elementwise | flops 32 | bytes 192 | tf_op jit(solution)/shard_map/convert_element_type | solution.py:545
  1.9 1.3 %convert_bitcast_fusion.cvar = f32[8,20]{1,0:T(8,128)} fusion(bf16[20,8]{0,1:T(8,128)(2,1)} %param.12), kind=kLoop, calls=%fused_computation | loop fusion | flops 160 | bytes 960 | tf_op jit(solution)/shard_map/convert_element_type | solution.py:545
  3.2 65.0 %shard_map.127 = (f32[64,256]{1,0:T(8,128)}, f32[4,16,512]{2,1,0:T(8,128)}, f32[8,8,256]{2,1,0:T(8,128)}, f32[8,256]{1,0:T(8,128)}, f32[16,128]{1,0:T(8,128)}) custom-call(f32[8,20]{1,0:T(8,128)} %convert_bitcast_fusion.cvar, f32[4,8]{1,0:T(4,128)} %convert_element_type.10.fvar, bf16[2,320,256]{2,1,0:T(8,128)(2,1)} %bitcast.11, bf16[16,64]{1,0:T(8,128)(2,1)} %clat.1, ...), custom_call_target="tpu_custom_call" | custom-call | tf_op jit(solution)/shard_map/pallas_call | solution.py:518
  68.1 1.7 %shard_map.128 = (f32[64,256]{1,0:T(8,128)}, f32[64,512]{1,0:T(8,128)}, f32[4,8]{1,0:T(4,128)}, f32[16,64]{1,0:T(8,128)}, f32[64,256]{1,0:T(8,128)}, /*index=5*/f32[8,20]{1,0:T(8,128)}) custom-call(f32[64,256]{1,0:T(8,128)} %get-tuple-element.17.flat, f32[4,16,512]{2,1,0:T(8,128)} %get-tuple-element.18.flon, f32[8,8,256]{2,1,0:T(8,128)} %get-tuple-element.19.fin, ...), custom_call_target="tpu_custom_call" | custom-call | tf_op jit(solution)/shard_map/pallas_call | solution.py:549
